TPU v7x, 128 devices: a whole 4x4x4 slice. The times are simulated.
128 devices in a mesh: brick: 16 (over z, x), slab: 8 (over y, core).
Axes of the slice: x: 4, y: 4, z: 4, core: 2. Of those that a mesh axis runs over, the one named last changes fastest.
Arguments:
- traces: bfloat16 [524288, 128], P(('brick', 'slab')), may hold values from -6 to 6
- owner: int32 [524288, 1], P(('brick', 'slab')), may hold values from 0 to 127; in each aligned block of 4096 rows (0 to 4095, 4096 to 8191, ...) at most 64 rows name the same one
- patch_node: int32 [524288], P(('brick', 'slab')), may hold values from 0 to 4095
- case_weights: int32 [16], replicated, may hold values from 1 to 9
- smoothing: float32 [512, 1024], P('brick', 'slab'), may hold values from 0.3 to 3
- links: int32 [4, 512, 1024], P(None, 'brick', 'slab'), may hold values 0 or 1
- prior: float32 [4096, 1024], P('brick', 'slab'), may hold values from -6 to 6
- stiffness: float32 [4096, 1024], P('brick', 'slab'), may hold values from 0.5 to 4
Outputs:
- smoothed: float32 [512, 1024], P('brick', 'slab')
- moved: float32 [4096, 1024], P('brick', 'slab')
Inputs may be any that keep to these rules, and one draw needn't show every extreme that they name: Among the 4096 face nodes of one device no owner is named more than 64 times, a bound that some block reaches.
All inputs are finite; a program needn't handle non-finite values. No bound on the sum of `links` on one device may be relied on, other than what follows from the above.
Results may differ from a plain program's by a relative error of at most 0.0003.
Values may be sent and summed in bfloat16 or wider, within the bound.
A program may use at most 64 MiB of HBM per device.

v0:
```python
import math

import jax
import jax.numpy as jnp
from jax import lax
from jax.sharding import PartitionSpec as P


def padded_2(block, sides, width):
    for axis, dim in sides:
        count = lax.axis_size(axis)
        forward = [(i, i + 1) for i in range(count - 1)]
        backward = [(target, source) for source, target in forward]
        low = lax.ppermute(
            lax.slice_in_dim(block, block.shape[dim] - width, None, axis=dim), axis, forward
        )
        high = lax.ppermute(lax.slice_in_dim(block, 0, width, axis=dim), axis, backward)
        block = jnp.concatenate([low, block, high], axis=dim)
    return block


def sweep_padded(padded, density, smoothing, links):
    beside = links[0] * padded[:-2, 1:-1] + links[1] * padded[2:, 1:-1]
    beside = beside + links[2] * padded[1:-1, :-2] + links[3] * padded[1:-1, 2:]
    degree = links[0] + links[1] + links[2] + links[3]
    return (density + smoothing * beside) / (1.0 + smoothing * degree)


def select_rows(keys, data, total):
    block_rows = math.gcd(total, 1024)

    def one_block(first):
        wanted = first * block_rows + jnp.arange(block_rows, dtype=jnp.int32)
        pick = (wanted[:, None] == keys[None, :]).astype(jnp.bfloat16)
        return jnp.dot(pick, data, preferred_element_type=jnp.float32)

    blocks = lax.map(one_block, jnp.arange(total // block_rows, dtype=jnp.int32))
    return blocks.reshape(total, data.shape[1])


def select_rows_by_slot(position, traces, slots):
    block_rows = math.gcd(slots, 1024)

    def one_block(first):
        wanted = first * block_rows + jnp.arange(block_rows, dtype=jnp.int32)
        pick = (wanted[:, None] == position[None, :]).astype(jnp.bfloat16)
        return jnp.dot(pick, traces, preferred_element_type=jnp.float32).astype(jnp.bfloat16)

    blocks = lax.map(one_block, jnp.arange(slots // block_rows, dtype=jnp.int32))
    return blocks.reshape(slots, traces.shape[1])


def local(traces, owner, patch_node, case_weights, smoothing, links, prior, stiffness):
    n_brick = lax.axis_size("brick")
    n_slab = lax.axis_size("slab")
    count = n_brick * n_slab
    rows, width = traces.shape
    capacity = 2 * rows // count
    slots = count * capacity
    patch_rows, patch_cols = smoothing.shape
    nodes_own = patch_rows * patch_cols
    target = owner[:, 0]
    onehot = (target[:, None] == jnp.arange(count, dtype=jnp.int32)[None, :]).astype(jnp.int32)
    before = jnp.cumsum(onehot, axis=0) - onehot
    place = jnp.sum(before * onehot, axis=1)
    position = target * capacity + place
    labels = jnp.full((slots,), -1, jnp.int32).at[position].set(patch_node)
    buffer = select_rows_by_slot(position, traces, slots)
    got_rows, got_ids = (
        lax.all_to_all(
            buffer.reshape(count, capacity, width),
            ("brick", "slab"),
            split_axis=0,
            concat_axis=0,
            tiled=True,
        ),
        lax.all_to_all(
            labels.reshape(count, capacity),
            ("brick", "slab"),
            split_axis=0,
            concat_axis=0,
            tiled=True,
        ),
    )
    got_ids = got_ids.reshape(-1)
    node_traces = select_rows(got_ids, got_rows.reshape(-1, width), nodes_own)
    cases = width // 8
    shaped = node_traces.reshape(nodes_own, cases, 8)
    terms = jnp.sum(shaped[:, :, :4] * shaped[:, :, 4:], axis=2)
    weights = case_weights.astype(jnp.float32)
    density = (jnp.dot(terms, weights, precision=lax.Precision.HIGHEST) / jnp.sum(weights)).reshape(
        patch_rows, patch_cols
    )
    linkf = links.astype(jnp.float32)
    values = density
    for turn in range(2):
        padded = padded_2(values, (("brick", 0), ("slab", 1)), 1)
        values = sweep_padded(padded, density, smoothing, linkf)
    safe_ids = jnp.where(got_ids < 0, nodes_own, got_ids)
    extended = jnp.concatenate([values.reshape(-1), jnp.zeros((1,), jnp.float32)])
    answer = extended[safe_ids].reshape(count, capacity)
    back = lax.all_to_all(answer, ("brick", "slab"), split_axis=0, concat_axis=0, tiled=True)
    shift = back.reshape(-1)[position]
    face_rows = rows // patch_cols
    start = prior.at[:face_rows, :].add(shift.reshape(face_rows, patch_cols))
    padded = padded_2(start, (("brick", 0), ("slab", 1)), 1)
    beside = padded[:-2, 1:-1] + padded[2:, 1:-1] + padded[1:-1, :-2] + padded[1:-1, 2:]
    moved = (stiffness * start + beside) / (stiffness + 4.0)
    return (values, moved)


def solution(mesh):
    in_specs = (
        P(("brick", "slab"), None),
        P(("brick", "slab"), None),
        P(("brick", "slab")),
        P(),
        P("brick", "slab"),
        P(None, "brick", "slab"),
        P("brick", "slab"),
        P("brick", "slab"),
    )
    out_specs = (P("brick", "slab"), P("brick", "slab"))
    return jax.shard_map(local, mesh=mesh, in_specs=in_specs, out_specs=out_specs, check_vma=False)
```

profile of v0, /device:TPU:1, one launch (start us, length us, event | category | flops | bytes accessed | tf_op | source)
XLA Modules:
  0.0 318.8 jit_solution(8230334578120112818)
XLA Ops:
  5.1 15.7 %scatter_custom_fusion = s32[8192]{0:T(1024)S(1)} fusion(s32[4096]{0:T(1024)S(1)} %bitcast.99, s32[4096]{0:T(1024)} %param.16, s32[]{:T(128)} %constant.67.clone.1), kind=kCustom, calls=%fused_computation.93 | custom fusion | bytes 33280 | tf_op jit(solution)/shard_map/scatter | solution.py:67
  21.5 11.5 %all-to-all-start = ((s32[128,1,64]{2,1,0:T(1,128)}), s32[128,1,64]{2,1,0:T(1,128)S(1)}, u32[]{:S(2)}, u32[]{:S(2)}) async-start(s32[128,1,64]{2,1,0:T(1,128)} %bitcast.11), calls=%async_computation | async-start | bytes 131072 | tf_op jit(solution)/shard_map/all_to_all | solution.py:77
  33.1 35.0 %while.22 = (s32[]{:T(128)}, bf16[8,1024,128]{2,1,0:T(8,128)(2,1)}, s32[8]{0:T(128)S(1)}, s32[4096]{0:T(1024)S(1)}, bf16[4096,128]{1,0:T(8,128)(2,1)S(1)}, /*index=5*/s32[]{:T(128)}, s32[1]{0:T(128)}) while((s32[]{:T(128)}, bf16[8,1024,128]{2,1,0:T(8,128)(2,1)}, s32[8]{0:T(128)S(1)}, s32[4096]{0:T(1024)S(1)}, bf16[4096,128]{1,0:T(8,128)(2,1)S(1)}, ...), condition=%wide.region_5.6_spmd, body=%wide.region_4.5_spmd.sunk | while | flops 1078068224 | bytes 1335913 | solution.py:49
  47.4 3.1 fusion.75
  60.6 3.1 fusion.75
  68.1 9.8 %all-to-all-start.1 = ((bf16[128,64,128]{2,1,0:T(8,128)(2,1)}), bf16[128,64,128]{2,1,0:T(8,128)(2,1)S(1)}, u32[]{:S(2)}, u32[]{:S(2)}) async-start(bf16[128,64,128]{2,1,0:T(8,128)(2,1)} %bitcast.88), calls=%async_computation.1 | async-start | bytes 4194304 | tf_op jit(solution)/shard_map/all_to_all | solution.py:70
  80.1 28.3 %all-to-all-done.1 = bf16[128,64,128]{2,1,0:T(8,128)(2,1)S(1)} async-done(((bf16[128,64,128]{2,1,0:T(8,128)(2,1)}), bf16[128,64,128]{2,1,0:T(8,128)(2,1)S(1)}, u32[]{:S(2)}, u32[]{:S(2)}) %all-to-all-start.1) | async-done | bytes 2097184 | tf_op jit(solution)/shard_map/all_to_all | solution.py:70
  108.4 66.4 %while.23 = (s32[]{:T(128)}, f32[4,1024,128]{1,0,2:T(4,128)}, s32[4]{0:T(128)S(1)}, s32[128,64]{1,0:T(8,128)}, bf16[8192,128]{1,0:T(8,128)(2,1)S(1)}, /*index=5*...) while((s32[]{:T(128)}, f32[4,1024,128]{1,0,2:T(4,128)}, s32[4]{0:T(128)S(1)}, ...), condition=%wide.wide.region_7.8_spmd, body=%wide.wide.region_6.7_spmd.sunk | while | flops 2155873280 | bytes 4759677 | solution.py:37
  109.5 4.5 %fusion.78 = f32[1,1024,128]{2,1,0:T(8,128)S(1)} fusion(bf16[8192,128]{1,0:T(8,128)(2,1)S(1)} %get-tuple-element.233, s32[8192]{0:T(1024)S(1)} %get-tuple-element.234, s32[1024]{0:T(1024)S(1)} %iota_add_fusion.6), kind=kOutput, calls=%fused_computation.15.clone.clone.1 | convolution fusion | flops 2155872256 | bytes 2658304 | tf_op jit(solution)/shard_map/while/body/eval_jaxpr/dot_general | solution.py:35
  114.4 10.5 %dynamic_update_slice.13 = f32[4,1024,128]{1,0,2:T(4,128)} dynamic-update-slice(f32[4,1024,128]{1,0,2:T(4,128)} %get-tuple-element.221, f32[1,1024,128]{1,0,2:T(1,128)S(1)} %copy.25, s32[]{:T(128)} %get-tuple-element.220, s32[]{:T(128)} %constant.65.clone.1..sunk, s32[]{:T(128)} %constant.65.clone.1..sunk) | dynamic-update-slice | bytes 1048580 | tf_op jit(solution)/shard_map/while/body/jit(dynamic_update_index_in_dim)/dynamic_update_slice | solution.py:37
  126.1 4.5 %fusion.78 = f32[1,1024,128]{2,1,0:T(8,128)S(1)} fusion(bf16[8192,128]{1,0:T(8,128)(2,1)S(1)} %get-tuple-element.233, s32[8192]{0:T(1024)S(1)} %get-tuple-element.234, s32[1024]{0:T(1024)S(1)} %iota_add_fusion.6), kind=kOutput, calls=%fused_computation.15.clone.clone.1 | convolution fusion | flops 2155872256 | bytes 2658304 | tf_op jit(solution)/shard_map/while/body/eval_jaxpr/dot_general | solution.py:35
  131.1 10.5 %dynamic_update_slice.13 = f32[4,1024,128]{1,0,2:T(4,128)} dynamic-update-slice(f32[4,1024,128]{1,0,2:T(4,128)} %get-tuple-element.221, f32[1,1024,128]{1,0,2:T(1,128)S(1)} %copy.25, s32[]{:T(128)} %get-tuple-element.220, s32[]{:T(128)} %constant.65.clone.1..sunk, s32[]{:T(128)} %constant.65.clone.1..sunk) | dynamic-update-slice | bytes 1048580 | tf_op jit(solution)/shard_map/while/body/jit(dynamic_update_index_in_dim)/dynamic_update_slice | solution.py:37
  142.7 4.5 %fusion.78 = f32[1,1024,128]{2,1,0:T(8,128)S(1)} fusion(bf16[8192,128]{1,0:T(8,128)(2,1)S(1)} %get-tuple-element.233, s32[8192]{0:T(1024)S(1)} %get-tuple-element.234, s32[1024]{0:T(1024)S(1)} %iota_add_fusion.6), kind=kOutput, calls=%fused_computation.15.clone.clone.1 | convolution fusion | flops 2155872256 | bytes 2658304 | tf_op jit(solution)/shard_map/while/body/eval_jaxpr/dot_general | solution.py:35
  147.7 10.5 %dynamic_update_slice.13 = f32[4,1024,128]{1,0,2:T(4,128)} dynamic-update-slice(f32[4,1024,128]{1,0,2:T(4,128)} %get-tuple-element.221, f32[1,1024,128]{1,0,2:T(1,128)S(1)} %copy.25, s32[]{:T(128)} %get-tuple-element.220, s32[]{:T(128)} %constant.65.clone.1..sunk, s32[]{:T(128)} %constant.65.clone.1..sunk) | dynamic-update-slice | bytes 1048580 | tf_op jit(solution)/shard_map/while/body/jit(dynamic_update_index_in_dim)/dynamic_update_slice | solution.py:37
  159.3 4.5 %fusion.78 = f32[1,1024,128]{2,1,0:T(8,128)S(1)} fusion(bf16[8192,128]{1,0:T(8,128)(2,1)S(1)} %get-tuple-element.233, s32[8192]{0:T(1024)S(1)} %get-tuple-element.234, s32[1024]{0:T(1024)S(1)} %iota_add_fusion.6), kind=kOutput, calls=%fused_computation.15.clone.clone.1 | convolution fusion | flops 2155872256 | bytes 2658304 | tf_op jit(solution)/shard_map/while/body/eval_jaxpr/dot_general | solution.py:35
  164.3 10.5 %dynamic_update_slice.13 = f32[4,1024,128]{1,0,2:T(4,128)} dynamic-update-slice(f32[4,1024,128]{1,0,2:T(4,128)} %get-tuple-element.221, f32[1,1024,128]{1,0,2:T(1,128)S(1)} %copy.25, s32[]{:T(128)} %get-tuple-element.220, s32[]{:T(128)} %constant.65.clone.1..sunk, s32[]{:T(128)} %constant.65.clone.1..sunk) | dynamic-update-slice | bytes 1048580 | tf_op jit(solution)/shard_map/while/body/jit(dynamic_update_index_in_dim)/dynamic_update_slice | solution.py:37
  201.5 3.3 %collective-permute-start.6 = (f32[34,1]{1,0:T(8,128)S(1)}, f32[34,1]{1,0:T(8,128)S(1)}, u32[]{:S(2)}, u32[]{:S(2)}) collective-permute-start(f32[34,1]{1,0:T(8,128)S(1)} %get-tuple-element.94), channel_id=1, source_target_pairs={{0,1},{1,2},{2,3},{3,4},{4,5},{5,6},{6,7},{8,9},{9,10},{10,11},{11... | collective-permute-start | bytes 416 | tf_op jit(solution)/shard_map/ppermute | solution.py:14
  206.8 3.1 collective-permute-done.7
  210.7 45.5 %gather_fusion = f32[8192]{0:T(1024)S(1)} fusion(f32[4097]{0:T(1024)S(1)} %pad_maximum_fusion.11, s32[8192]{0:T(1024)S(1)} %broadcast_clamp_fusion), kind=kCustom, calls=%fused_computation | custom fusion | bytes 98304 | tf_op jit(solution)/shard_map/gather | solution.py:101
  257.0 9.8 %all-to-all-start.2 = ((f32[128,1,64]{2,1,0:T(1,128)}), f32[128,1,64]{2,1,0:T(1,128)S(1)}, u32[]{:S(2)}, u32[]{:S(2)}) async-start(f32[128,1,64]{2,1,0:T(1,128)} %bitcast.26), calls=%async_computation.2 | async-start | bytes 131072 | tf_op jit(solution)/shard_map/all_to_all | solution.py:102
  266.8 9.5 %all-to-all-done.2 = f32[128,1,64]{2,1,0:T(1,128)S(1)} async-done(((f32[128,1,64]{2,1,0:T(1,128)}), f32[128,1,64]{2,1,0:T(1,128)S(1)}, u32[]{:S(2)}, u32[]{:S(2)}) %all-to-all-start.2) | async-done | bytes 32800 | tf_op jit(solution)/shard_map/all_to_all | solution.py:102
  277.7 23.0 %gather_fusion.1 = f32[4096]{0:T(1024)S(1)} fusion(f32[8192]{0:T(1024)S(1)} %reshape.124, s32[4096]{0:T(1024)S(1)} %broadcast_clamp_fusion.1), kind=kCustom, calls=%fused_computation.1 | custom fusion | bytes 49152 | tf_op jit(solution)/shard_map/gather | solution.py:103
  307.4 4.2 %collective-permute-start.10 = (f32[258,1]{1,0:T(8,128)S(1)}, f32[258,1]{1,0:T(8,128)S(1)}, u32[]{:S(2)}, u32[]{:S(2)}) collective-permute-start(f32[258,1]{1,0:T(8,128)S(1)} %get-tuple-element.92), channel_id=1, source_target_pairs={{0,1},{1,2},{2,3},{3,4},{4,5},{5,6},{6,7},{8,9},{9,10},{10,11},{11... | collective-permute-start | bytes 3104 | tf_op jit(solution)/shard_map/ppermute | solution.py:14
  313.6 4.4 %collective-permute-done.11 = f32[258,1]{1,0:T(8,128)S(1)} collective-permute-done((f32[258,1]{1,0:T(8,128)S(1)}, f32[258,1]{1,0:T(8,128)S(1)}, u32[]{:S(2)}, u32[]{:S(2)}) %collective-permute-start.11) | collective-permute-done | bytes 1064 | tf_op jit(solution)/shard_map/ppermute | solution.py:17
  (121 shorter events, 75.4 us)
Async XLA Ops:
  2.4 1.3 copy-start.2
  3.6 29.5 %copy-start.8 = (bf16[4096,128]{1,0:T(8,128)(2,1)S(1)}, bf16[4096,128]{1,0:T(8,128)(2,1)}, u32[]{:S(2)}) copy-start(bf16[4096,128]{1,0:T(8,128)(2,1)} %param.14) | copy-start | bytes 3145732
  21.5 46.5 %all-to-all-start = ((s32[128,1,64]{2,1,0:T(1,128)}), s32[128,1,64]{2,1,0:T(1,128)S(1)}, u32[]{:S(2)}, u32[]{:S(2)}) async-start(s32[128,1,64]{2,1,0:T(1,128)} %bitcast.11), calls=%async_computation | async-start | bytes 131072 | tf_op jit(solution)/shard_map/all_to_all | solution.py:77
  68.1 11.2 %copy-start.1 = (s32[128,1,64]{2,1,0:T(1,128)}, s32[128,1,64]{2,1,0:T(1,128)S(1)}, u32[]{:S(2)}) copy-start(s32[128,1,64]{2,1,0:T(1,128)S(1)} %all-to-all-done) | copy-start | bytes 98308
  68.1 9.8 %copy-start.4 = (s32[4,32,128]{2,1,0:T(8,128)S(1)}, s32[4,32,128]{2,1,0:T(8,128)}, u32[]{:S(2)}) copy-start(s32[4,32,128]{2,1,0:T(8,128)} %param.19) | copy-start | bytes 196612
  68.1 9.8 %copy-start.7 = (s32[16]{0:T(128)S(1)}, s32[16]{0:T(128)}, u32[]{:S(2)}) copy-start(s32[16]{0:T(128)} %param.17) | copy-start | bytes 196
  68.1 40.3 %all-to-all-start.1 = ((bf16[128,64,128]{2,1,0:T(8,128)(2,1)}), bf16[128,64,128]{2,1,0:T(8,128)(2,1)S(1)}, u32[]{:S(2)}, u32[]{:S(2)}) async-start(bf16[128,64,128]{2,1,0:T(8,128)(2,1)} %bitcast.88), calls=%async_computation.1 | async-start | bytes 4194304 | tf_op jit(solution)/shard_map/all_to_all | solution.py:70
  177.5 16.4 %copy-start.5 = (f32[32,128]{1,0:T(8,128)S(1)}, f32[32,128]{1,0:T(8,128)}, u32[]{:S(2)}) copy-start(f32[32,128]{1,0:T(8,128)} %param.18) | copy-start | bytes 49156
  179.3 4.0 %collective-permute-start = (f32[1,128]{1,0:T(1,128)S(1)}, f32[1,128]{1,0:T(1,128)S(1)}, u32[]{:S(2)}, u32[]{:S(2)}) collective-permute-start(f32[1,128]{1,0:T(1,128)S(1)} %get-tuple-element.100), channel_id=1, source_target_pairs={{0,8},{8,16},{16,24},{24,32},{32,40},{40,48},{48,56},{56,64},{64,7... | collective-permute-start | bytes 1544 | tf_op jit(solution)/shard_map/ppermute | solution.py:14
  181.3 4.3 %collective-permute-start.1 = (f32[1,128]{1,0:T(1,128)S(1)}, f32[1,128]{1,0:T(1,128)S(1)}, u32[]{:S(2)}, u32[]{:S(2)}) collective-permute-start(f32[1,128]{1,0:T(1,128)S(1)} %get-tuple-element.101), channel_id=1, source_target_pairs={{8,0},{16,8},{24,16},{32,24},{40,32},{48,40},{56,48},{64,56},{72,6... | collective-permute-start | bytes 1544 | tf_op jit(solution)/shard_map/ppermute | solution.py:17
  185.7 5.9 %collective-permute-start.2 = (f32[34,1]{1,0:T(8,128)S(1)}, f32[34,1]{1,0:T(8,128)S(1)}, u32[]{:S(2)}, u32[]{:S(2)}) collective-permute-start(f32[34,1]{1,0:T(8,128)S(1)} %get-tuple-element.96), channel_id=1, source_target_pairs={{0,1},{1,2},{2,3},{3,4},{4,5},{5,6},{6,7},{8,9},{9,10},{10,11},{11... | collective-permute-start | bytes 416 | tf_op jit(solution)/shard_map/ppermute | solution.py:14
  188.8 5.1 %collective-permute-start.3 = (f32[34,1]{1,0:T(8,128)S(1)}, f32[34,1]{1,0:T(8,128)S(1)}, u32[]{:S(2)}, u32[]{:S(2)}) collective-permute-start(f32[34,1]{1,0:T(8,128)S(1)} %get-tuple-element.97), channel_id=1, source_target_pairs={{1,0},{2,1},{3,2},{4,3},{5,4},{6,5},{7,6},{9,8},{10,9},{11,10},{12... | collective-permute-start | bytes 416 | tf_op jit(solution)/shard_map/ppermute | solution.py:17
  194.0 4.5 %collective-permute-start.4 = (f32[1,128]{1,0:T(1,128)S(1)}, f32[1,128]{1,0:T(1,128)S(1)}, u32[]{:S(2)}, u32[]{:S(2)}) collective-permute-start(f32[1,128]{1,0:T(1,128)S(1)} %get-tuple-element.98), channel_id=1, source_target_pairs={{0,8},{8,16},{16,24},{24,32},{32,40},{40,48},{48,56},{56,64},{64,7... | collective-permute-start | bytes 1544 | tf_op jit(solution)/shard_map/ppermute | solution.py:14
  197.1 4.3 %collective-permute-start.5 = (f32[1,128]{1,0:T(1,128)S(1)}, f32[1,128]{1,0:T(1,128)S(1)}, u32[]{:S(2)}, u32[]{:S(2)}) collective-permute-start(f32[1,128]{1,0:T(1,128)S(1)} %get-tuple-element.99), channel_id=1, source_target_pairs={{8,0},{16,8},{24,16},{32,24},{40,32},{48,40},{56,48},{64,56},{72,6... | collective-permute-start | bytes 1544 | tf_op jit(solution)/shard_map/ppermute | solution.py:17
  201.5 5.3 %collective-permute-start.6 = (f32[34,1]{1,0:T(8,128)S(1)}, f32[34,1]{1,0:T(8,128)S(1)}, u32[]{:S(2)}, u32[]{:S(2)}) collective-permute-start(f32[34,1]{1,0:T(8,128)S(1)} %get-tuple-element.94), channel_id=1, source_target_pairs={{0,1},{1,2},{2,3},{3,4},{4,5},{5,6},{6,7},{8,9},{9,10},{10,11},{11... | collective-permute-start | bytes 416 | tf_op jit(solution)/shard_map/ppermute | solution.py:14
  204.8 5.1 %collective-permute-start.7 = (f32[34,1]{1,0:T(8,128)S(1)}, f32[34,1]{1,0:T(8,128)S(1)}, u32[]{:S(2)}, u32[]{:S(2)}) collective-permute-start(f32[34,1]{1,0:T(8,128)S(1)} %get-tuple-element.95), channel_id=1, source_target_pairs={{1,0},{2,1},{3,2},{4,3},{5,4},{6,5},{7,6},{9,8},{10,9},{11,10},{12... | collective-permute-start | bytes 416 | tf_op jit(solution)/shard_map/ppermute | solution.py:17
  210.7 45.6 %copy-start.6 = (f32[32,128]{1,0:T(8,128)}, f32[32,128]{1,0:T(8,128)S(1)}, u32[]{:S(2)}) copy-start(f32[32,128]{1,0:T(8,128)S(1)} %fusion.35) | copy-start | bytes 49156
  257.0 19.3 %all-to-all-start.2 = ((f32[128,1,64]{2,1,0:T(1,128)}), f32[128,1,64]{2,1,0:T(1,128)S(1)}, u32[]{:S(2)}, u32[]{:S(2)}) async-start(f32[128,1,64]{2,1,0:T(1,128)} %bitcast.26), calls=%async_computation.2 | async-start | bytes 131072 | tf_op jit(solution)/shard_map/all_to_all | solution.py:102
  277.7 23.0 %copy-start = (f32[256,128]{1,0:T(8,128)S(1)}, f32[256,128]{1,0:T(8,128)}, u32[]{:S(2)}) copy-start(f32[256,128]{1,0:T(8,128)} %param.20) | copy-start | bytes 393220
  277.7 40.2 %copy-start.3 = (f32[256,128]{1,0:T(8,128)S(1)}, f32[256,128]{1,0:T(8,128)}, u32[]{:S(2)}) copy-start(f32[256,128]{1,0:T(8,128)} %param.21) | copy-start | bytes 393220
  300.8 3.5 %collective-permute-start.8 = (f32[1,128]{1,0:T(1,128)S(1)}, f32[1,128]{1,0:T(1,128)S(1)}, u32[]{:S(2)}, u32[]{:S(2)}) collective-permute-start(f32[1,128]{1,0:T(1,128)S(1)} %slice.201), channel_id=1, source_target_pairs={{0,8},{8,16},{16,24},{24,32},{32,40},{40,48},{48,56},{56,64},{64,7... | collective-permute-start | bytes 1544 | tf_op jit(solution)/shard_map/ppermute | solution.py:14
  303.0 4.3 %collective-permute-start.9 = (f32[1,128]{1,0:T(1,128)S(1)}, f32[1,128]{1,0:T(1,128)S(1)}, u32[]{:S(2)}, u32[]{:S(2)}) collective-permute-start(f32[1,128]{1,0:T(1,128)S(1)} %slice.202), channel_id=1, source_target_pairs={{8,0},{16,8},{24,16},{32,24},{40,32},{48,40},{56,48},{64,56},{72,6... | collective-permute-start | bytes 1544 | tf_op jit(solution)/shard_map/ppermute | solution.py:17
  307.4 6.2 %collective-permute-start.10 = (f32[258,1]{1,0:T(8,128)S(1)}, f32[258,1]{1,0:T(8,128)S(1)}, u32[]{:S(2)}, u32[]{:S(2)}) collective-permute-start(f32[258,1]{1,0:T(8,128)S(1)} %get-tuple-element.92), channel_id=1, source_target_pairs={{0,1},{1,2},{2,3},{3,4},{4,5},{5,6},{6,7},{8,9},{9,10},{10,11},{11... | collective-permute-start | bytes 3104 | tf_op jit(solution)/shard_map/ppermute | solution.py:14
  311.6 6.3 %collective-permute-start.11 = (f32[258,1]{1,0:T(8,128)S(1)}, f32[258,1]{1,0:T(8,128)S(1)}, u32[]{:S(2)}, u32[]{:S(2)}) collective-permute-start(f32[258,1]{1,0:T(8,128)S(1)} %get-tuple-element.93), channel_id=1, source_target_pairs={{1,0},{2,1},{3,2},{4,3},{5,4},{6,5},{7,6},{9,8},{10,9},{11,10},{12... | collective-permute-start | bytes 3104 | tf_op jit(solution)/shard_map/ppermute | solution.py:17
where the time goes:
time: 322 us; the launch traced here: 319 us
  local copies, waits for them, and re-layouts  143 us (44%)
  starting transfers between devices  59.4 us (18%)
  waiting for transfers between devices  55.8 us (17%)
  matrix products  43.3 us (13%)
  other arithmetic  8.73 us (3%)
  loops' own time  7.5 us (2%)
    gather x1, local copies, waits for them, and re-layouts, local(): answer = extended[safe_ids].reshape(count, capacity)  45.5 us
    dynamic_update_slice x8, local copies, waits for them, and re-layouts, select_rows(): lax.map(one_block, jnp.arange(total // block_rows, dtype=jnp.int32))  43.8 us
    all_to_all x1, waiting for transfers between devices, local(): lax.all_to_all(buffer.reshape(count, capacity, width), ('brick', 'slab'),...  28.3 us
    dot_general x8, matrix products, one_block(): jnp.dot(pick, traces, preferred_element_type=jnp.float32)  24.9 us
    gather x1, local copies, waits for them, and re-layouts, local(): shift = back.reshape(-1)[position]  23 us
    dot_general x4, matrix products, one_block(): return jnp.dot(pick, data, preferred_element_type=jnp.float32)  18.2 us
    ppermute x6, waiting for transfers between devices, padded_2(): lax.ppermute(lax.slice_in_dim(block, 0, width, axis=dim), axis, backward)  18 us
    ppermute x6, starting transfers between devices, padded_2(): lax.ppermute(lax.slice_in_dim(block, block.shape[dim] - width, None, axis...  17.9 us
  transfers between devices with their start and end apart: 15, of which 8 were waited for; matrix products, arithmetic and copies ran while one was open for 10% of the time, Pallas kernels for 0%

commit v1 on v0

v1 whole, which is shorter than its diff:
```python
import functools

import jax
import jax.numpy as jnp
from jax import lax
from jax.experimental import pallas as pl
from jax.experimental.pallas import tpu as pltpu
from jax.sharding import PartitionSpec as P

MESH = pl.DeviceIdType.MESH
F32 = jnp.float32
BF16 = jnp.bfloat16
I32 = jnp.int32

NB = 16
NS = 8
ND = NB * NS
ROWS = 4096
CAP = 64
W = 128
STRIDE = 37
UNSTRIDE = 45
STEPS = 8
PER = ND // STEPS
DLO = 512
CLO = 1024
CHUNK = PER * CAP


def onehot(sub, row):
    return jnp.where(sub == row, 1.0, 0.0).astype(BF16)


def lanes(x, index):
    return jnp.take_along_axis(x, index, axis=1, mode="promise_in_bounds")


def lookup(table, nrows, hi, lo):
    out = jnp.zeros(hi.shape, F32)
    for r in range(nrows):
        row = jnp.broadcast_to(table[r : r + 1, :], (8, W))
        out = jnp.where(hi == r, lanes(row, lo), out)
    return out


def kernel(
    tr_hbm, own_ref, node_ref, cw_ref, sm_ref, lk_ref, prior_ref, st_ref,
    sm_out, mv_out,
    tr, ot, plo, hib, rhs, sendbuf, recv, ints, plc, labl, r1, r2, ids, idrel, idp, nhib,
    qlo, rr, acc, sheet, vone, vtwo, hg, hv, ans, q1, q2, fin, finp, start, vu, vd, vl, vr, cl, cr, cpl, cpr,
    in_sem, tsend, trecv, lsend, lrecv, l2send, l2recv, hsend, hrecv, asend, arecv, a2send, a2recv, vsend, vrecv,
):
    b = lax.axis_index("brick")
    s = lax.axis_index("slab")
    me = b * NS + s

    bar = pltpu.get_barrier_semaphore()

    def greet(i, _):
        t = lax.rem(me + i, ND)
        pl.semaphore_signal(bar, inc=1, device_id=(t // NS, lax.rem(t, NS)), device_id_type=MESH)
        return 0

    lax.fori_loop(1, ND, greet, 0, unroll=4)
    pltpu.make_async_copy(tr_hbm, tr, in_sem).start()

    own = own_ref[...]
    order = ((own - me + ND) * UNSTRIDE) & (ND - 1)
    slabwise = (own & (NS - 1)) * NB + (own >> 3)
    ints[0] = order & 7
    ints[1] = slabwise
    sub128 = lax.broadcasted_iota(I32, (W, W), 0)

    def fill_ot(a, _):
        col = pl.ds(pl.multiple_of(a * W, W), W)
        ot[0:W, col] = onehot(sub128, ints[1, pl.ds(a, 1), :])
        return 0

    lax.fori_loop(0, 32, fill_ot, 0, unroll=4)
    upper = jnp.where(
        lax.broadcasted_iota(I32, (256, 256), 0) < lax.broadcasted_iota(I32, (256, 256), 1), 1.0, 0.0
    ).astype(BF16)
    carry = jnp.zeros((W, 1), F32)
    for k in range(16):
        block = ot[0:W, k * 256 : (k + 1) * 256]
        blockf = block.astype(F32)
        before = jnp.dot(block, upper, preferred_element_type=F32) + carry
        place = jnp.sum(before * blockf, axis=0, keepdims=True).astype(I32)
        plc[2 * k : 2 * k + 1, :] = place[:, :W]
        plc[2 * k + 1 : 2 * k + 2, :] = place[:, W:]
        carry = before[:, 255:256] + blockf[:, 255:256]

    sub64 = lax.broadcasted_iota(I32, (CAP, W), 0)

    def fill_plo(a, _):
        col = pl.ds(pl.multiple_of(a * W, W), W)
        spot = onehot(sub64, plc[pl.ds(a, 1), :])
        low = jnp.broadcast_to(ints[0, pl.ds(a, 1), :], (16, W))
        for q in range(8):
            pick = jnp.where(low == q, 1.0, 0.0).astype(BF16)
            plo[q * CAP : (q + 1) * CAP, col] = spot * jnp.concatenate([pick] * 4, axis=0)
        return 0

    lax.fori_loop(0, 32, fill_plo, 0, unroll=2)
    turned = jnp.concatenate(
        [(order >> 3).astype(F32), plc[...].astype(F32), jnp.zeros((64, W), F32)], axis=0
    ).T
    for a in range(32):
        hib[a * W : (a + 1) * W, :] = jnp.broadcast_to(turned[:, a : a + 1], (W, W)).astype(BF16)

    pl.semaphore_wait(bar, ND - 1)
    pltpu.make_async_copy(tr_hbm, tr, in_sem).wait()

    up = (lax.rem(b + NB - 1, NB), s)
    down = (lax.rem(b + 1, NB), s)
    left = (b, lax.rem(s + NS - 1, NS))
    right = (b, lax.rem(s + 1, NS))

    def rcopy(src, dst, ss, rs, dev):
        return pltpu.make_async_remote_copy(
            src_ref=src, dst_ref=dst, send_sem=ss, recv_sem=rs, device_id=dev, device_id_type=MESH
        )

    lane8 = lax.broadcasted_iota(I32, (8, W), 1)

    def early_copies():
        return [
            rcopy(prior_ref.at[pl.ds(248, 8)], vu, vsend.at[0], vrecv.at[0], down),
            rcopy(cpl, cr, vsend.at[1], vrecv.at[1], left),
            rcopy(cpr, cl, vsend.at[2], vrecv.at[2], right),
        ]

    def early():
        first = jnp.zeros((8, W), F32)
        last = jnp.zeros((8, W), F32)
        for a in range(32):
            tile = prior_ref[a * 8 : (a + 1) * 8, :]
            first = jnp.where(lane8 == a, jnp.broadcast_to(tile[:, 0:1], (8, W)), first)
            last = jnp.where(lane8 == a, jnp.broadcast_to(tile[:, W - 1 : W], (8, W)), last)
        cpl[...] = first
        cpr[...] = last
        for c in early_copies():
            c.start()

    def stage1_copy(d):
        to = lax.rem(s + d, NS)
        return rcopy(
            labl.at[pl.ds(to * NB, NB)], r1.at[pl.ds(s * NB, NB)], lsend, lrecv, (b, to)
        )

    def labels_stage1():
        node1 = node_ref[...] + 1
        ints[2] = node1 >> 6
        ints[3] = node1 & 63

        def scale(a, _):
            col = pl.ds(pl.multiple_of(a * W, W), W)
            block = ot[0:W, col]
            low = ints[3, pl.ds(a, 1), :].astype(F32)
            high = ints[2, pl.ds(a, 1), :].astype(F32)
            low = jnp.broadcast_to(low, (16, W)).astype(BF16)
            high = jnp.broadcast_to(high, (16, W)).astype(BF16)
            ot[W : 2 * W, col] = block * jnp.concatenate([low] * 8, axis=0)
            ot[0:W, col] = block * jnp.concatenate([high] * 8, axis=0)
            return 0

        lax.fori_loop(0, 32, scale, 0, unroll=2)
        spots = jnp.concatenate([plc[...].astype(F32), jnp.zeros((96, W), F32)], axis=0).T
        lane64 = (lax.broadcasted_iota(I32, (W, W), 1) & (CAP - 1)).astype(F32)
        for a in range(32):
            rhs[a * W : (a + 1) * W, 0:W] = jnp.where(
                jnp.broadcast_to(spots[:, a : a + 1], (W, W)) == lane64, 1.0, 0.0
            ).astype(BF16)
        out = jnp.dot(ot[...], rhs[:, 0:W], preferred_element_type=F32)
        labl[...] = (out[0:W, :] * 64.0 + out[W : 2 * W, :]).astype(I32)
        r1[pl.ds(pl.multiple_of(s * NB, NB), NB), :] = labl[pl.ds(pl.multiple_of(s * NB, NB), NB), :]

        def go(d, _):
            stage1_copy(d).start()
            return 0

        lax.fori_loop(1, NS, go, 0)

    def stage2_copy(d):
        to = lax.rem(b + d, NB)
        return rcopy(
            r2.at[pl.ds(to * NS, NS)], ids.at[pl.ds(b * NS, NS)], l2send, l2recv, (to, s)
        )

    def labels_stage2():
        pltpu.make_async_copy(labl.at[pl.ds(0, 7 * NB)], r1.at[pl.ds(0, 7 * NB)], lrecv).wait()
        for t in range(NB):
            r2[t * NS : (t + 1) * NS, :] = r1[pl.ds(t, NS, stride=NB), :]
        mine = pl.ds(pl.multiple_of(b * NS, NS), NS)
        ids[mine, :] = r2[mine, :]

        def go(d, _):
            stage2_copy(d).start()
            return 0

        lax.fori_loop(1, NB, go, 0)

    def trace_copy(i):
        t = lax.rem(me + STRIDE * i, ND)
        return rcopy(
            sendbuf.at[i], recv.at[i], tsend, trecv.at[i // PER], (t // NS, lax.rem(t, NS))
        )

    def dispatch(j, _):
        want0 = jnp.full((256, W), 2 * j, I32).astype(F32).astype(BF16)
        want1 = jnp.full((256, W), 2 * j + 1, I32).astype(F32).astype(BF16)

        def mask(k, _):
            rows = pl.ds(pl.multiple_of(k * 256, 256), 256)
            group = hib[rows, :]
            data = tr[rows, :]
            rhs[rows, 0:W] = jnp.where(group == want0, data, jnp.zeros_like(data))
            rhs[rows, W : 2 * W] = jnp.where(group == want1, data, jnp.zeros_like(data))
            return 0

        lax.fori_loop(0, 16, mask, 0, unroll=2)
        out = jnp.dot(plo[...], rhs[...], preferred_element_type=F32).astype(BF16)
        for h in range(2):
            sendbuf[pl.ds(PER * j + 8 * h, 8)] = out[:, h * W : (h + 1) * W].reshape(8, CAP, W)

        @pl.when(j == 0)
        def _():
            pltpu.make_async_copy(sendbuf.at[0], recv.at[0], trecv.at[0]).start()

        def go(i, _):
            trace_copy(PER * j + i).start()
            return 0

        lax.fori_loop(jnp.where(j == 0, 1, 0), PER, go, 0)

        @pl.when(j == 0)
        def _():
            labels_stage1()
            early()

        @pl.when(j == 2)
        def _():
            labels_stage2()

        return 0

    lax.fori_loop(0, STEPS, dispatch, 0)

    pltpu.make_async_copy(r2.at[pl.ds(0, 15 * NS)], ids.at[pl.ds(0, 15 * NS)], l2recv).wait()

    def reorder(i, _):
        src = lax.rem(me - STRIDE * i + ND * STRIDE, ND)
        idrel[pl.ds(i, 1), :] = ids[pl.ds(src, 1), :]
        return 0

    lax.fori_loop(0, ND, reorder, 0, unroll=8)
    lane64w = lax.broadcasted_iota(I32, (64, W), 1)
    idp[...] = jnp.where(lane64w < CAP, idrel[pl.ds(0, 64, stride=2), :], idrel[pl.ds(1, 64, stride=2), :]) - 1
    quarters = jnp.concatenate([(idp[...] >> 10).astype(F32), jnp.zeros((64, W), F32)], axis=0).T
    for a in range(64):
        nhib[a * W : (a + 1) * W, :] = jnp.broadcast_to(quarters[:, a : a + 1], (W, W)).astype(BF16)
    acc[...] = jnp.zeros_like(acc)

    def combine(k, _):
        pltpu.make_async_copy(
            sendbuf.at[pl.ds(0, PER)], recv.at[pl.ds(PER * k, PER)], trecv.at[k]
        ).wait()
        for p in range(8):
            node = idp[pl.ds(8 * k + p, 1), :] & (CLO - 1)
            spot = onehot(sub64, node & 63)
            high = jnp.broadcast_to(node >> 6, (16, W))
            for q in range(16):
                pick = jnp.where(high == q, 1.0, 0.0).astype(BF16)
                qlo[q * CAP : (q + 1) * CAP, p * W : (p + 1) * W] = spot * jnp.concatenate([pick] * 4, axis=0)

        def mask(i, _):
            rows = pl.ds(pl.multiple_of(i * 256, 256), 256)
            group = nhib[pl.ds(pl.multiple_of(k * CHUNK + i * 256, 256), 256), :]
            data = recv[pl.ds(PER * k + 4 * i, 4)].reshape(256, W)
            for h in range(4):
                rr[rows, h * W : (h + 1) * W] = jnp.where(
                    group == jnp.full((256, W), h, BF16), data, jnp.zeros_like(data)
                )
            return 0

        lax.fori_loop(0, CHUNK // 256, mask, 0)
        acc[...] += jnp.dot(qlo[...], rr[...], preferred_element_type=F32)
        return 0

    lax.fori_loop(0, STEPS, combine, 0)

    lane1 = lax.broadcasted_iota(I32, (16, W), 1)
    weights = jnp.zeros((16, W), F32)
    total = jnp.float32(0.0)
    for c in range(16):
        wc = cw_ref[c].astype(F32)
        total = total + wc
        weights = jnp.where((lane1 >> 3) == c, wc, weights)
    weights = jnp.where((lane1 & 7) < 4, weights, 0.0).astype(BF16)
    contract = (((1,), (1,)), ((), ()))
    for h in range(4):
        x = acc[:, h * W : (h + 1) * W]
        prod = x * pltpu.roll(x, W - 4, axis=1)
        coarse = prod.astype(BF16)
        fine = (prod - coarse.astype(F32)).astype(BF16)
        d = lax.dot_general(weights, coarse, contract, preferred_element_type=F32)
        d = d + lax.dot_general(weights, fine, contract, preferred_element_type=F32)
        for q in range(8):
            sheet[8 * h + q : 8 * h + q + 1, :] = d[0:1, q * W : (q + 1) * W]
    sheet[...] = sheet[...] / total

    def halo_copies(src, box, n):
        return [
            rcopy(src.at[pl.ds(0, 8)], box.at[1, pl.ds(0, 8)], hsend.at[n], hrecv.at[n], up),
            rcopy(src.at[pl.ds(24, 8)], box.at[0, pl.ds(24, 8)], hsend.at[n + 1], hrecv.at[n + 1], down),
            rcopy(src, box.at[3], hsend.at[n + 2], hrecv.at[n + 2], left),
            rcopy(src, box.at[2], hsend.at[n + 3], hrecv.at[n + 3], right),
        ]

    row32 = lax.broadcasted_iota(I32, (32, W), 0)
    lane32 = lax.broadcasted_iota(I32, (32, W), 1)
    smooth = sm_ref[...]
    link = [lk_ref[i].astype(F32) for i in range(4)]
    degree = 1.0 + smooth * (link[0] + link[1] + link[2] + link[3])

    def sweep(src, box, n):
        copies = halo_copies(src, box, n)
        for c in copies:
            c.start()
        for c in copies:
            c.wait()
        v = src[...]
        above = jnp.where(b == 0, 0.0, jnp.broadcast_to(box[0, 31:32, :], (32, W)))
        below = jnp.where(b == NB - 1, 0.0, jnp.broadcast_to(box[1, 0:1, :], (32, W)))
        before = jnp.where(s == 0, 0.0, pltpu.roll(box[2], 1, axis=1))
        after = jnp.where(s == NS - 1, 0.0, pltpu.roll(box[3], W - 1, axis=1))
        above = jnp.where(row32 == 0, above, pltpu.roll(v, 1, axis=0))
        below = jnp.where(row32 == 31, below, pltpu.roll(v, 31, axis=0))
        before = jnp.where(lane32 == 0, before, pltpu.roll(v, 1, axis=1))
        after = jnp.where(lane32 == W - 1, after, pltpu.roll(v, W - 1, axis=1))
        beside = link[0] * above + link[1] * below + link[2] * before + link[3] * after
        return (sheet[...] + smooth * beside) / degree

    vone[...] = sweep(sheet, hg, 0)
    vtwo[...] = sweep(vone, hv, 4)
    sm_out[...] = vtwo[...]

    def answer(t, _):
        rows = pl.ds(pl.multiple_of(t * 8, 8), 8)
        node = ids[rows, :] - 1
        ans[rows, :] = lookup(vtwo, 32, node >> 7, node & (W - 1))
        return 0

    lax.fori_loop(0, NB, answer, 0)

    def back1_copy(d):
        to = lax.rem(b + d, NB)
        return rcopy(ans.at[pl.ds(to * NS, NS)], q1.at[pl.ds(b * NS, NS)], asend, arecv, (to, s))

    def go1(d, _):
        back1_copy(d).start()
        return 0

    lax.fori_loop(1, NB, go1, 0)
    mine = pl.ds(pl.multiple_of(b * NS, NS), NS)
    q1[mine, :] = ans[mine, :]
    pltpu.make_async_copy(ans.at[pl.ds(0, 15 * NS)], q1.at[pl.ds(0, 15 * NS)], arecv).wait()
    for t in range(NS):
        q2[t * NB : (t + 1) * NB, :] = q1[pl.ds(t, NB, stride=NS), :]

    def back2_copy(d):
        to = lax.rem(s + d, NS)
        return rcopy(q2.at[pl.ds(to * NB, NB)], fin.at[pl.ds(s * NB, NB)], a2send, a2recv, (b, to))

    def go2(d, _):
        back2_copy(d).start()
        return 0

    lax.fori_loop(1, NS, go2, 0)
    mine = pl.ds(pl.multiple_of(s * NB, NB), NB)
    fin[mine, :] = q2[mine, :]
    pltpu.make_async_copy(q2.at[pl.ds(0, 7 * NB)], fin.at[pl.ds(0, 7 * NB)], a2recv).wait()

    finp[...] = jnp.where(lane64w < CAP, fin[pl.ds(0, 64, stride=2), :], fin[pl.ds(1, 64, stride=2), :])
    start[...] = prior_ref[...]

    def place_shift(t, _):
        rows = pl.ds(pl.multiple_of(t * 8, 8), 8)
        m = ints[1, rows, :]
        shift = lookup(finp, 64, m >> 1, ((m & 1) << 6) + plc[rows, :])
        start[rows, :] = start[rows, :] + shift
        return 0

    lax.fori_loop(0, 4, place_shift, 0)

    late = [
        rcopy(start.at[pl.ds(0, 8)], vd, vsend.at[3], vrecv.at[3], up),
        rcopy(start.at[pl.ds(0, 32)], vr, vsend.at[4], vrecv.at[4], left),
        rcopy(start.at[pl.ds(0, 32)], vl, vsend.at[5], vrecv.at[5], right),
    ]
    for c in late:
        c.start()
    for c in early_copies():
        c.wait()
    for c in late:
        c.wait()
    x = start[...]
    firsts = [pltpu.roll(vl[...], 1, axis=1)]
    lasts = [pltpu.roll(vr[...], W - 1, axis=1)]
    for a in range(4, 32):
        firsts.append(jnp.broadcast_to(cl[:, a : a + 1], (8, W)))
        lasts.append(jnp.broadcast_to(cr[:, a : a + 1], (8, W)))
    before = jnp.where(s == 0, 0.0, jnp.concatenate(firsts, axis=0))
    after = jnp.where(s == NS - 1, 0.0, jnp.concatenate(lasts, axis=0))
    above = jnp.where(b == 0, 0.0, jnp.broadcast_to(vu[7:8, :], (256, W)))
    below = jnp.where(b == NB - 1, 0.0, jnp.broadcast_to(vd[0:1, :], (256, W)))
    row256 = lax.broadcasted_iota(I32, (256, W), 0)
    lane256 = lax.broadcasted_iota(I32, (256, W), 1)
    above = jnp.where(row256 == 0, above, pltpu.roll(x, 1, axis=0))
    below = jnp.where(row256 == 255, below, pltpu.roll(x, 255, axis=0))
    before = jnp.where(lane256 == 0, before, pltpu.roll(x, 1, axis=1))
    after = jnp.where(lane256 == W - 1, after, pltpu.roll(x, W - 1, axis=1))
    stiff = st_ref[...]
    mv_out[...] = (stiff * x + (above + below + before + after)) / (stiff + 4.0)

    pltpu.make_async_copy(sendbuf.at[pl.ds(0, ND - 1)], recv.at[pl.ds(0, ND - 1)], tsend).wait()
    pltpu.make_async_copy(labl.at[pl.ds(0, 7 * NB)], r1.at[pl.ds(0, 7 * NB)], lsend).wait()
    pltpu.make_async_copy(r2.at[pl.ds(0, 15 * NS)], ids.at[pl.ds(0, 15 * NS)], l2send).wait()
    pltpu.make_async_copy(ans.at[pl.ds(0, 15 * NS)], q1.at[pl.ds(0, 15 * NS)], asend).wait()
    pltpu.make_async_copy(q2.at[pl.ds(0, 7 * NB)], fin.at[pl.ds(0, 7 * NB)], a2send).wait()


def local(traces, owner, patch_node, case_weights, smoothing, links, prior, stiffness):
    vmem = pl.BlockSpec(memory_space=pltpu.VMEM)
    V = pltpu.VMEM
    dma = pltpu.SemaphoreType.DMA
    return pl.pallas_call(
        kernel,
        out_shape=(
            jax.ShapeDtypeStruct((32, W), F32),
            jax.ShapeDtypeStruct((256, W), F32),
        ),
        in_specs=[pl.BlockSpec(memory_space=pl.ANY), vmem, vmem, pl.BlockSpec(memory_space=pltpu.SMEM)] + [vmem] * 4,
        out_specs=(vmem, vmem),
        scratch_shapes=[
            V((ROWS, W), BF16),
            V((2 * W, ROWS), BF16),
            V((DLO, ROWS), BF16),
            V((ROWS, W), BF16),
            V((ROWS, 2 * W), BF16),
            V((ND, CAP, W), BF16),
            V((ND, CAP, W), BF16),
            V((4, 32, W), I32),
            V((32, W), I32),
            V((ND, W), I32),
            V((ND, W), I32),
            V((ND, W), I32),
            V((ND, W), I32),
            V((ND, W), I32),
            V((ND // 2, W), I32),
            V((ND * CAP, W), BF16),
            V((CLO, CHUNK), BF16),
            V((CHUNK, 4 * W), BF16),
            V((CLO, 4 * W), F32),
            V((32, W), F32),
            V((32, W), F32),
            V((32, W), F32),
            V((4, 32, W), F32),
            V((4, 32, W), F32),
            V((ND, W), F32),
            V((ND, W), F32),
            V((ND, W), F32),
            V((ND, W), F32),
            V((ND // 2, W), F32),
            V((256, W), F32),
            V((8, W), F32),
            V((8, W), F32),
            V((32, W), F32),
            V((32, W), F32),
            V((8, W), F32),
            V((8, W), F32),
            V((8, W), F32),
            V((8, W), F32),
            dma, dma, dma((STEPS,)), dma, dma, dma, dma, dma((8,)), dma((8,)), dma, dma, dma, dma, dma((6,)), dma((6,)),
        ],
        compiler_params=pltpu.CompilerParams(
            collective_id=0, has_side_effects=True, vmem_limit_bytes=56 << 20
        ),
    )(
        traces, owner.reshape(32, W), patch_node.reshape(32, W), case_weights, smoothing, links, prior, stiffness
    )


def solution(mesh):
    in_specs = (
        P(("brick", "slab"), None),
        P(("brick", "slab"), None),
        P(("brick", "slab")),
        P(),
        P("brick", "slab"),
        P(None, "brick", "slab"),
        P("brick", "slab"),
        P("brick", "slab"),
    )
    out_specs = (P("brick", "slab"), P("brick", "slab"))
    return jax.shard_map(local, mesh=mesh, in_specs=in_specs, out_specs=out_specs, check_vma=False)
```

time: 322 us -> 77.8 us (0.24)
  local copies, waits for them, and re-layouts: 143 us -> 2.89 us
  Pallas kernels: 0 us -> 74 us
  starting transfers between devices: 59.4 us -> 0 us
  waiting for transfers between devices: 55.8 us -> 0 us
  matrix products: 43.3 us -> 0 us
  other arithmetic: 8.73 us -> 0 us
  loops' own time: 7.5 us -> 0 us
    pallas_call x0 -> x1, Pallas kernels: none -> 74 us  [local(): pl.pallas_call(kernel, out_shape=(jax.ShapeDtypeStruct((32, W), F32), jax...]
    gather x2 -> x0, local copies, waits for them, and re-layouts: 68.6 us -> none  [the longest x1 45.5 us: local(): answer = extended[safe_ids].reshape(count, capacity)]
    dynamic_update_slice x8 -> x0, local copies, waits for them, and re-layouts: 43.8 us -> none  [select_rows(): lax.map(one_block, jnp.arange(total // block_rows, dtype=jnp.int32))]
    dot_general x13 -> x0, matrix products: 43.3 us -> none  [the longest x8 24.9 us: one_block(): jnp.dot(pick, traces, preferred_element_type=jnp.float32)]
    all_to_all x3 -> x0, waiting for transfers between devices: 37.8 us -> none  [the longest x1 28.3 us: local(): lax.all_to_all(buffer.reshape(count, capacity, width), ('brick', 'slab'),...]
    all_to_all x3 -> x0, starting transfers between devices: 31.1 us -> none  [the longest x1 11.5 us: local(): lax.all_to_all(labels.reshape(count, capacity), ('brick', 'slab'), split_...]
    ppermute x12 -> x0, starting transfers between devices: 28.3 us -> none  [the longest x6 17.9 us: padded_2(): lax.ppermute(lax.slice_in_dim(block, block.shape[dim] - width, None, axis...]
    ppermute x12 -> x0, waiting for transfers between devices: 18 us -> none  [the longest x6 18 us: padded_2(): lax.ppermute(lax.slice_in_dim(block, 0, width, axis=dim), axis, backward)]
  transfers between devices with their start and end apart: 15 -> 0, of which waited for: 8 -> 0; matrix products, arithmetic and copies ran while one was open for 10% -> 0% of each run, Pallas kernels for 0% -> 0%
where the time goes in v1:
time: 77.8 us; the launch traced here: 77.5 us
  Pallas kernels  74 us (95%)
  local copies, waits for them, and re-layouts  2.89 us (4%)
    pallas_call x1, Pallas kernels, local(): pl.pallas_call(kernel, out_shape=(jax.ShapeDtypeStruct((32, W), F32), jax...  74 us
    unnamed x2, local copies, waits for them, and re-layouts  2.89 us

profile of v1, /device:TPU:1, one launch (start us, length us, event | category | flops | bytes accessed | tf_op | source)
XLA Modules:
  0.0 77.5 jit_solution(13771332336938999457)
XLA Ops:
  0.6 74.0 %shard_map.95 = (f32[32,128]{1,0:T(8,128)}, f32[256,128]{1,0:T(8,128)}) custom-call(bf16[4096,128]{1,0:T(8,128)(2,1)} %tr_hbm.1, s32[32,128]{1,0:T(8,128)} %bitcast.2, s32[32,128]{1,0:T(8,128)} %bitcast.3, s32[16]{0:T(128)} %cw_ref.1, f32[32,128]{1,0:T(8,128)} %sm_ref.1, s32[4,32,128]{2,1,0:T(8,128)} %lk_ref.1, f32[256,128]{1,0:T(8,128)} %prior_ref.1, ...), custom_call_target="tpu_custom_call" | custom-call | tf_op jit(solution)/shard_map/pallas_call | solution.py:437
  74.6 1.3 %copy.12 = f32[32,128]{1,0:T(8,128)} copy(f32[32,128]{1,0:T(8,128)} %get-tuple-element.4) | data formatting | bytes 32768
  76.0 1.6 %copy.13 = f32[256,128]{1,0:T(8,128)} copy(f32[256,128]{1,0:T(8,128)} %get-tuple-element.5) | data formatting | bytes 262144

commit v2 on v1

v2 whole, which is shorter than its diff:
```python
import functools

import jax
import jax.numpy as jnp
from jax import lax
from jax.experimental import pallas as pl
from jax.experimental.pallas import tpu as pltpu
from jax.sharding import PartitionSpec as P

MESH = pl.DeviceIdType.MESH
F32 = jnp.float32
BF16 = jnp.bfloat16
I32 = jnp.int32

NB = 16
NS = 8
ND = NB * NS
ROWS = 4096
CAP = 64
W = 128
STRIDE = 37
UNSTRIDE = 45
BACK = 21
STEPS = 8
PER = ND // STEPS
DLO = 512
CLO = 1024
CHUNK = PER * CAP


def onehot(sub, row):
    return jnp.where(sub == row, 1.0, 0.0).astype(BF16)


def lanes(x, index):
    return jnp.take_along_axis(x, index, axis=1, mode="promise_in_bounds")


def lookup(table, nrows, hi, lo):
    out = jnp.zeros(hi.shape, F32)
    for r in range(nrows):
        row = jnp.broadcast_to(table[r : r + 1, :], (8, W))
        out = jnp.where(hi == r, lanes(row, lo), out)
    return out


def kernel(
    tr_hbm, own_ref, node_ref, cw_ref, sm_ref, lk_ref, prior_ref, st_ref,
    sm_out, mv_out,
    tr, ot, plo, hib, rhs, sendbuf, recv, ints, plc, labl, r1, r2, ids, idrel, idp, nhib,
    qlo, acc, sheet, vtwo, sides, ends, pairs, ans, msg, back, mine3, other3, tables, codes, eu, ed, el, er, vu, vd, vl, vr,
    in_sem, tsend, trecv, lsend, lrecv, l2send, l2recv, hsend, hrecv, asend, arecv, csend, crecv, vsend, vrecv,
):
    b = lax.axis_index("brick")
    s = lax.axis_index("slab")
    me = b * NS + s

    bar = pltpu.get_barrier_semaphore()

    def greet(i, _):
        t = lax.rem(me + i, ND)
        pl.semaphore_signal(bar, inc=1, device_id=(t // NS, lax.rem(t, NS)), device_id_type=MESH)
        return 0

    lax.fori_loop(1, ND, greet, 0, unroll=4)
    pltpu.make_async_copy(tr_hbm, tr, in_sem).start()

    own = own_ref[...]
    order = ((own - me + ND) * UNSTRIDE - 1) & (ND - 1)
    slabwise = (own & (NS - 1)) * NB + (own >> 3)
    ints[0] = order & 7
    ints[1] = slabwise
    sub128 = lax.broadcasted_iota(I32, (W, W), 0)

    def fill_ot(a, _):
        col = pl.ds(pl.multiple_of(a * W, W), W)
        ot[0:W, col] = onehot(sub128, ints[1, pl.ds(a, 1), :])
        return 0

    lax.fori_loop(0, 32, fill_ot, 0, unroll=4)
    upper = jnp.where(
        lax.broadcasted_iota(I32, (256, 256), 0) < lax.broadcasted_iota(I32, (256, 256), 1), 1.0, 0.0
    ).astype(BF16)
    carry = jnp.zeros((W, 1), F32)
    for k in range(16):
        block = ot[0:W, k * 256 : (k + 1) * 256]
        blockf = block.astype(F32)
        before = jnp.dot(block, upper, preferred_element_type=F32) + carry
        place = jnp.sum(before * blockf, axis=0, keepdims=True).astype(I32)
        plc[2 * k : 2 * k + 1, :] = place[:, :W]
        plc[2 * k + 1 : 2 * k + 2, :] = place[:, W:]
        carry = before[:, 255:256] + blockf[:, 255:256]

    codes[...] = own * CAP + plc[...]

    sub64 = lax.broadcasted_iota(I32, (CAP, W), 0)

    def fill_plo(a, _):
        col = pl.ds(pl.multiple_of(a * W, W), W)
        spot = onehot(sub64, plc[pl.ds(a, 1), :])
        low = jnp.broadcast_to(ints[0, pl.ds(a, 1), :], (16, W))
        for q in range(8):
            pick = jnp.where(low == q, 1.0, 0.0).astype(BF16)
            plo[q * CAP : (q + 1) * CAP, col] = spot * jnp.concatenate([pick] * 4, axis=0)
        return 0

    lax.fori_loop(0, 32, fill_plo, 0, unroll=2)
    turned = jnp.concatenate(
        [(order >> 3).astype(F32), plc[...].astype(F32), jnp.zeros((64, W), F32)], axis=0
    ).T
    for a in range(32):
        hib[a * W : (a + 1) * W, :] = jnp.broadcast_to(turned[:, a : a + 1], (W, W)).astype(BF16)

    pltpu.make_async_copy(tr_hbm, tr, in_sem).wait()

    up = (lax.rem(b + NB - 1, NB), s)
    down = (lax.rem(b + 1, NB), s)
    left = (b, lax.rem(s + NS - 1, NS))
    right = (b, lax.rem(s + 1, NS))

    def rcopy(src, dst, ss, rs, dev):
        return pltpu.make_async_remote_copy(
            src_ref=src, dst_ref=dst, send_sem=ss, recv_sem=rs, device_id=dev, device_id_type=MESH
        )

    lane8 = lax.broadcasted_iota(I32, (8, W), 1)

    def early_copies():
        return [
            rcopy(eu, vd, vsend.at[0], vrecv.at[0], up),
            rcopy(ed, vu, vsend.at[1], vrecv.at[1], down),
            rcopy(el, vr, vsend.at[2], vrecv.at[2], left),
            rcopy(er, vl, vsend.at[3], vrecv.at[3], right),
        ]

    def early():
        eu[...] = jnp.zeros_like(eu)
        ed[...] = jnp.zeros_like(ed)
        eu[0:1, :] = sm_ref[0:1, :]
        ed[0:1, :] = sm_ref[31:32, :]
        for k in range(4):
            eu[k + 1 : k + 2, :] = lk_ref[k, 0:1, :].astype(F32)
            ed[k + 1 : k + 2, :] = lk_ref[k, 31:32, :].astype(F32)
        eu[5:6, :] = codes[0:1, :].astype(F32)
        eu[6:7, :] = prior_ref[0:1, :]
        ed[5:6, :] = prior_ref[255:256, :]
        columns = [prior_ref[a * 8 : (a + 1) * 8, :] for a in range(32)]
        columns += [sm_ref[a * 8 : (a + 1) * 8, :] for a in range(4)]
        for k in range(4):
            columns += [lk_ref[k, a * 8 : (a + 1) * 8, :].astype(F32) for a in range(4)]
        columns += [codes[a * 8 : (a + 1) * 8, :].astype(F32) for a in range(4)]
        first = jnp.zeros((8, W), F32)
        last = jnp.zeros((8, W), F32)
        for a, tile in enumerate(columns):
            first = jnp.where(lane8 == a, jnp.broadcast_to(tile[:, 0:1], (8, W)), first)
            last = jnp.where(lane8 == a, jnp.broadcast_to(tile[:, W - 1 : W], (8, W)), last)
        el[...] = first
        er[...] = last
        for c in early_copies():
            c.start()

    def stage1_copy(d):
        to = lax.rem(s + d, NS)
        return rcopy(
            labl.at[pl.ds(to * NB, NB)], r1.at[pl.ds(s * NB, NB)], lsend, lrecv, (b, to)
        )

    def labels_stage1():
        node1 = node_ref[...] + 1
        ints[2] = node1 >> 6
        ints[3] = node1 & 63

        def scale(a, _):
            col = pl.ds(pl.multiple_of(a * W, W), W)
            block = ot[0:W, col]
            low = ints[3, pl.ds(a, 1), :].astype(F32)
            high = ints[2, pl.ds(a, 1), :].astype(F32)
            low = jnp.broadcast_to(low, (16, W)).astype(BF16)
            high = jnp.broadcast_to(high, (16, W)).astype(BF16)
            ot[W : 2 * W, col] = block * jnp.concatenate([low] * 8, axis=0)
            ot[0:W, col] = block * jnp.concatenate([high] * 8, axis=0)
            return 0

        lax.fori_loop(0, 32, scale, 0, unroll=2)
        spots = jnp.concatenate([plc[...].astype(F32), jnp.zeros((96, W), F32)], axis=0).T
        lane64 = (lax.broadcasted_iota(I32, (W, W), 1) & (CAP - 1)).astype(F32)
        for a in range(32):
            rhs[a * W : (a + 1) * W, 0:W] = jnp.where(
                jnp.broadcast_to(spots[:, a : a + 1], (W, W)) == lane64, 1.0, 0.0
            ).astype(BF16)
        out = jnp.dot(ot[...], rhs[:, 0:W], preferred_element_type=F32)
        labl[...] = (out[0:W, :] * 64.0 + out[W : 2 * W, :]).astype(I32)
        r1[pl.ds(pl.multiple_of(s * NB, NB), NB), :] = labl[pl.ds(pl.multiple_of(s * NB, NB), NB), :]

        pl.semaphore_wait(bar, ND - 1)

        def go(d, _):
            stage1_copy(d).start()
            return 0

        lax.fori_loop(1, NS, go, 0)

    def stage2_copy(d):
        to = lax.rem(b + d, NB)
        return rcopy(
            r2.at[pl.ds(to * NS, NS)], ids.at[pl.ds(b * NS, NS)], l2send, l2recv, (to, s)
        )

    def labels_stage2():
        pltpu.make_async_copy(labl.at[pl.ds(0, 7 * NB)], r1.at[pl.ds(0, 7 * NB)], lrecv).wait()
        for t in range(NB):
            r2[t * NS : (t + 1) * NS, :] = r1[pl.ds(t, NS, stride=NB), :]
        mine = pl.ds(pl.multiple_of(b * NS, NS), NS)
        ids[mine, :] = r2[mine, :]

        def go(d, _):
            stage2_copy(d).start()
            return 0

        lax.fori_loop(1, NB, go, 0)

    def trace_copy(i):
        t = lax.rem(me + STRIDE * (i + 1), ND)
        return rcopy(
            sendbuf.at[i], recv.at[i], tsend, trecv.at[i // PER], (t // NS, lax.rem(t, NS))
        )

    def fill_step(j):
        group = hib[...]
        data = tr[...]
        masked = [
            jnp.where(group == jnp.full((ROWS, W), 2 * j + h, I32).astype(F32).astype(BF16), data, jnp.zeros_like(data))
            for h in range(2)
        ]
        out = jnp.dot(plo[...], jnp.concatenate(masked, axis=1), preferred_element_type=F32).astype(BF16)
        for h in range(2):
            sendbuf[pl.ds(PER * j + 8 * h, 8)] = out[:, h * W : (h + 1) * W].reshape(8, CAP, W)

    def dispatch(j, _):
        def go(i, _):
            trace_copy(PER * (j - 1) + i).start()
            return 0

        lax.fori_loop(0, PER, go, 0)
        fill_step(j)

        @pl.when(j == 1)
        def _():
            labels_stage2()

        @pl.when(j == 4)
        def _():
            early()

        return 0

    labels_stage1()
    fill_step(0)
    lax.fori_loop(1, STEPS, dispatch, 0)

    def last(i, _):
        trace_copy(PER * (STEPS - 1) + i).start()
        return 0

    lax.fori_loop(0, PER - 1, last, 0)
    pltpu.make_async_copy(sendbuf.at[ND - 1], recv.at[ND - 1], trecv.at[STEPS - 1]).start()

    pltpu.make_async_copy(r2.at[pl.ds(0, 15 * NS)], ids.at[pl.ds(0, 15 * NS)], l2recv).wait()

    def reorder(i, _):
        src = lax.rem(me - STRIDE * (i + 1) + ND * STRIDE, ND)
        idrel[pl.ds(i, 1), :] = ids[pl.ds(src, 1), :]
        return 0

    lax.fori_loop(0, ND, reorder, 0, unroll=8)
    lane64w = lax.broadcasted_iota(I32, (64, W), 1)
    pairs[...] = jnp.where(lane64w < CAP, ids[pl.ds(0, 64, stride=2), :], ids[pl.ds(1, 64, stride=2), :]) - 1
    idp[...] = jnp.where(lane64w < CAP, idrel[pl.ds(0, 64, stride=2), :], idrel[pl.ds(1, 64, stride=2), :]) - 1
    quarters = jnp.concatenate([(idp[...] >> 10).astype(F32), jnp.zeros((64, W), F32)], axis=0).T
    for a in range(64):
        nhib[a * W : (a + 1) * W, :] = jnp.broadcast_to(quarters[:, a : a + 1], (W, W)).astype(BF16)
    acc[...] = jnp.zeros_like(acc)

    def combine(k, _):
        pltpu.make_async_copy(
            sendbuf.at[pl.ds(0, PER)], recv.at[pl.ds(PER * k, PER)], trecv.at[k]
        ).wait()
        for p in range(8):
            node = idp[pl.ds(8 * k + p, 1), :] & (CLO - 1)
            spot = onehot(sub64, node & 63)
            high = jnp.broadcast_to(node >> 6, (16, W))
            for q in range(16):
                pick = jnp.where(high == q, 1.0, 0.0).astype(BF16)
                qlo[q * CAP : (q + 1) * CAP, p * W : (p + 1) * W] = spot * jnp.concatenate([pick] * 4, axis=0)

        group = nhib[pl.ds(pl.multiple_of(k * CHUNK, CHUNK), CHUNK), :]
        data = recv[pl.ds(PER * k, PER)].reshape(CHUNK, W)
        masked = [
            jnp.where(group == jnp.full((CHUNK, W), h, BF16), data, jnp.zeros_like(data)) for h in range(4)
        ]
        acc[...] += jnp.dot(qlo[...], jnp.concatenate(masked, axis=1), preferred_element_type=F32)
        return 0

    lax.fori_loop(0, STEPS, combine, 0)

    lane1 = lax.broadcasted_iota(I32, (16, W), 1)
    weights = jnp.zeros((16, W), F32)
    total = jnp.float32(0.0)
    for c in range(16):
        wc = cw_ref[c].astype(F32)
        total = total + wc
        weights = jnp.where((lane1 >> 3) == c, wc, weights)
    weights = jnp.where((lane1 & 7) < 4, weights, 0.0).astype(BF16)
    contract = (((1,), (1,)), ((), ()))
    for h in range(4):
        x = acc[:, h * W : (h + 1) * W]
        prod = x * pltpu.roll(x, W - 4, axis=1)
        coarse = prod.astype(BF16)
        fine = (prod - coarse.astype(F32)).astype(BF16)
        d = lax.dot_general(weights, coarse, contract, preferred_element_type=F32)
        d = d + lax.dot_general(weights, fine, contract, preferred_element_type=F32)
        for q in range(8):
            sheet[8 * h + q : 8 * h + q + 1, :] = d[0:1, q * W : (q + 1) * W]
    sheet[...] = sheet[...] / total

    upleft = (lax.rem(b + NB - 1, NB), lax.rem(s + NS - 1, NS))
    upright = (lax.rem(b + NB - 1, NB), lax.rem(s + 1, NS))
    downleft = (lax.rem(b + 1, NB), lax.rem(s + NS - 1, NS))
    downright = (lax.rem(b + 1, NB), lax.rem(s + 1, NS))
    top = sheet.at[pl.ds(0, 8)]
    bottom = sheet.at[pl.ds(24, 8)]
    swaps = [
        rcopy(top, ends.at[5], hsend.at[5], hrecv.at[5], upleft),
        rcopy(top, ends.at[4], hsend.at[4], hrecv.at[4], upright),
        rcopy(bottom, ends.at[3], hsend.at[3], hrecv.at[3], downleft),
        rcopy(bottom, ends.at[2], hsend.at[2], hrecv.at[2], downright),
        rcopy(top, ends.at[1], hsend.at[1], hrecv.at[1], up),
        rcopy(bottom, ends.at[0], hsend.at[0], hrecv.at[0], down),
        rcopy(sheet, sides.at[1], hsend.at[6], hrecv.at[6], left),
        rcopy(sheet, sides.at[0], hsend.at[7], hrecv.at[7], right),
    ]
    for c in swaps:
        c.start()
    row32 = lax.broadcasted_iota(I32, (32, W), 0)
    lane32 = lax.broadcasted_iota(I32, (32, W), 1)
    lane1r = lax.broadcasted_iota(I32, (1, W), 1)
    smooth = sm_ref[...]
    link = [lk_ref[i].astype(F32) for i in range(4)]
    no_up, no_down, no_left, no_right = b == 0, b == NB - 1, s == 0, s == NS - 1

    def relax(v, smooth, link, above, below, before, after):
        beside = link[0] * above + link[1] * below + link[2] * before + link[3] * after
        return (v + smooth * beside) / (1.0 + smooth * (link[0] + link[1] + link[2] + link[3]))

    def column(tile, k):
        parts = [jnp.broadcast_to(tile[:, 32 + 4 * k + t : 33 + 4 * k + t], (8, W)) for t in range(4)]
        return jnp.concatenate(parts, axis=0)

    for c in early_copies():
        c.wait()
    coef_left = [column(vl[...], k) for k in range(5)]
    coef_right = [column(vr[...], k) for k in range(5)]
    g = sheet[...]
    for c in swaps:
        c.wait()
    gu6 = jnp.where(no_up, 0.0, ends[0, 6:7, :])
    gu7 = jnp.where(no_up, 0.0, ends[0, 7:8, :])
    gd0 = jnp.where(no_down, 0.0, ends[1, 0:1, :])
    gd1 = jnp.where(no_down, 0.0, ends[1, 1:2, :])
    gul = jnp.where(no_up | no_left, 0.0, ends[2, 7:8, :])
    gur = jnp.where(no_up | no_right, 0.0, ends[3, 7:8, :])
    gdl = jnp.where(no_down | no_left, 0.0, ends[4, 0:1, :])
    gdr = jnp.where(no_down | no_right, 0.0, ends[5, 0:1, :])
    gl = jnp.where(no_left, 0.0, sides[0])
    gr = jnp.where(no_right, 0.0, sides[1])

    def shifted(v, above, below, before, after):
        return (
            jnp.where(row32 == 0, above, pltpu.roll(v, 1, axis=0)),
            jnp.where(row32 == 31, below, pltpu.roll(v, 31, axis=0)),
            jnp.where(lane32 == 0, pltpu.roll(before, 1, axis=1), pltpu.roll(v, 1, axis=1)),
            jnp.where(lane32 == W - 1, pltpu.roll(after, W - 1, axis=1), pltpu.roll(v, W - 1, axis=1)),
        )

    def shifted_row(v, before, after):
        return (
            jnp.where(lane1r == 0, pltpu.roll(before, 1, axis=1), pltpu.roll(v, 1, axis=1)),
            jnp.where(lane1r == W - 1, pltpu.roll(after, W - 1, axis=1), pltpu.roll(v, W - 1, axis=1)),
        )

    one = relax(g, smooth, link, *shifted(g, gu7, gd0, gl, gr))
    one_up = relax(
        gu7, vu[0:1, :], [vu[k : k + 1, :] for k in range(1, 5)], gu6, g[0:1, :], *shifted_row(gu7, gul, gur)
    )
    one_down = relax(
        gd0, vd[0:1, :], [vd[k : k + 1, :] for k in range(1, 5)], g[31:32, :], gd1, *shifted_row(gd0, gdl, gdr)
    )
    one_left = relax(gl, coef_left[0], coef_left[1:], *shifted(gl, gul, gdl, gl, g))
    one_right = relax(gr, coef_right[0], coef_right[1:], *shifted(gr, gur, gdr, g, gr))
    one_up = jnp.where(no_up, 0.0, one_up)
    one_down = jnp.where(no_down, 0.0, one_down)
    one_left = jnp.where(no_left, 0.0, one_left)
    one_right = jnp.where(no_right, 0.0, one_right)
    beside = shifted(one, one_up, one_down, one_left, one_right)
    sumside = link[0] * beside[0] + link[1] * beside[1] + link[2] * beside[2] + link[3] * beside[3]
    two = (g + smooth * sumside) / (1.0 + smooth * (link[0] + link[1] + link[2] + link[3]))
    vtwo[...] = two
    sm_out[...] = two

    def answer(t, _):
        rows = pl.ds(pl.multiple_of(t * 8, 8), 8)
        node = pairs[rows, :]
        ans[rows, :] = lookup(vtwo, 32, node >> 7, node & (W - 1))
        return 0

    lax.fori_loop(0, 8, answer, 0)
    pair = ans[...]
    msg[pl.ds(0, 64, stride=8), :] = pair
    msg[pl.ds(1, 64, stride=8), :] = pltpu.roll(pair, 60, axis=0)
    msg[pl.ds(2, 64, stride=8), :] = jnp.where(
        lane64w < CAP, pltpu.roll(pair, 63, axis=0), pltpu.roll(pair, 1, axis=0)
    )
    core = lax.rem(s, 2)
    chip = b * 4 + s // 2

    def back_copy(i):
        t = lax.rem(chip + BACK * i, ND // 2)
        return rcopy(
            msg.at[pl.ds(t * 8, 8)], back.at[pl.ds(chip * 8, 8)], asend, arecv, (t // 4, 2 * lax.rem(t, 4) + core)
        )

    def go1(i, _):
        back_copy(i).start()
        return 0

    lax.fori_loop(1, ND // 2, go1, 0)
    here = pl.ds(pl.multiple_of(chip * 8, 8), 8)
    back[here, :] = msg[here, :]
    pltpu.make_async_copy(msg.at[pl.ds(0, 63 * 8)], back.at[pl.ds(0, 63 * 8)], arecv).wait()
    for k in range(3):
        mine3[k] = back[pl.ds(k, 64, stride=8), :]
    swap = rcopy(mine3, other3, csend, crecv, (b, s + 1 - 2 * core))
    swap.start()
    swap.wait()
    def halves(k, half):
        own_part, other_part = mine3[k], other3[k]
        even = jnp.where(core == 0, own_part, other_part)
        odd = jnp.where(core == 0, other_part, own_part)
        even = jnp.where(half == 0, even, pltpu.roll(even, CAP, axis=1))
        odd = jnp.where(half == 1, odd, pltpu.roll(odd, CAP, axis=1))
        return jnp.where(lane64w < CAP, even, odd)

    partner_table = halves(0, 1 - core)
    far_table = halves(2, 1 - core)
    tables[0] = halves(0, core)
    tables[1] = halves(1, core)
    tables[2] = jnp.where(core == 0, far_table, partner_table)
    tables[3] = jnp.where(core == 0, partner_table, far_table)

    def answered(k, code):
        return lookup(tables.at[k], 64, code >> 7, code & (W - 1))

    shift = jnp.concatenate([answered(0, codes[a * 8 : (a + 1) * 8, :]) for a in range(4)], axis=0)
    shift_down = answered(1, vd[...].astype(I32))[5:6, :]
    lanes_late = lane8 < 4
    edge_left = vl[...]
    edge_right = vr[...]
    edge_left = edge_left + jnp.where(
        lanes_late, pltpu.roll(answered(2, edge_left.astype(I32)), W - 52, axis=1), 0.0
    )
    edge_right = edge_right + jnp.where(
        lanes_late, pltpu.roll(answered(3, edge_right.astype(I32)), W - 52, axis=1), 0.0
    )
    x = jnp.concatenate([prior_ref[0:32, :] + shift, prior_ref[32:256, :]], axis=0)
    before = jnp.concatenate([jnp.broadcast_to(edge_left[:, a : a + 1], (8, W)) for a in range(32)], axis=0)
    after = jnp.concatenate([jnp.broadcast_to(edge_right[:, a : a + 1], (8, W)) for a in range(32)], axis=0)
    before = jnp.where(no_left, 0.0, before)
    after = jnp.where(no_right, 0.0, after)
    above = jnp.where(no_up, 0.0, vu[5:6, :])
    below = jnp.where(no_down, 0.0, vd[6:7, :] + shift_down)
    row256 = lax.broadcasted_iota(I32, (256, W), 0)
    lane256 = lax.broadcasted_iota(I32, (256, W), 1)
    above = jnp.where(row256 == 0, above, pltpu.roll(x, 1, axis=0))
    below = jnp.where(row256 == 255, below, pltpu.roll(x, 255, axis=0))
    before = jnp.where(lane256 == 0, before, pltpu.roll(x, 1, axis=1))
    after = jnp.where(lane256 == W - 1, after, pltpu.roll(x, W - 1, axis=1))
    stiff = st_ref[...]
    mv_out[...] = (stiff * x + (above + below + before + after)) / (stiff + 4.0)

    pltpu.make_async_copy(sendbuf.at[pl.ds(0, ND - 1)], recv.at[pl.ds(0, ND - 1)], tsend).wait()
    pltpu.make_async_copy(labl.at[pl.ds(0, 7 * NB)], r1.at[pl.ds(0, 7 * NB)], lsend).wait()
    pltpu.make_async_copy(r2.at[pl.ds(0, 15 * NS)], ids.at[pl.ds(0, 15 * NS)], l2send).wait()
    pltpu.make_async_copy(msg.at[pl.ds(0, 63 * 8)], back.at[pl.ds(0, 63 * 8)], asend).wait()


def local(traces, owner, patch_node, case_weights, smoothing, links, prior, stiffness):
    vmem = pl.BlockSpec(memory_space=pltpu.VMEM)
    V = pltpu.VMEM
    dma = pltpu.SemaphoreType.DMA
    return pl.pallas_call(
        kernel,
        out_shape=(
            jax.ShapeDtypeStruct((32, W), F32),
            jax.ShapeDtypeStruct((256, W), F32),
        ),
        in_specs=[pl.BlockSpec(memory_space=pl.ANY), vmem, vmem, pl.BlockSpec(memory_space=pltpu.SMEM)] + [vmem] * 4,
        out_specs=(vmem, vmem),
        scratch_shapes=[
            V((ROWS, W), BF16),
            V((2 * W, ROWS), BF16),
            V((DLO, ROWS), BF16),
            V((ROWS, W), BF16),
            V((ROWS, 2 * W), BF16),
            V((ND, CAP, W), BF16),
            V((ND, CAP, W), BF16),
            V((4, 32, W), I32),
            V((32, W), I32),
            V((ND, W), I32),
            V((ND, W), I32),
            V((ND, W), I32),
            V((ND, W), I32),
            V((ND, W), I32),
            V((ND // 2, W), I32),
            V((ND * CAP, W), BF16),
            V((CLO, CHUNK), BF16),
            V((CLO, 4 * W), F32),
            V((32, W), F32),
            V((32, W), F32),
            V((2, 32, W), F32),
            V((6, 8, W), F32),
            V((ND // 2, W), I32),
            V((ND // 2, W), F32),
            V((ND * 4, W), F32),
            V((ND * 4, W), F32),
            V((3, ND // 2, W), F32),
            V((3, ND // 2, W), F32),
            V((4, ND // 2, W), F32),
            V((32, W), I32),
            V((8, W), F32),
            V((8, W), F32),
            V((8, W), F32),
            V((8, W), F32),
            V((8, W), F32),
            V((8, W), F32),
            V((8, W), F32),
            V((8, W), F32),
            dma, dma, dma((STEPS,)), dma, dma, dma, dma, dma((8,)), dma((8,)), dma, dma, dma, dma, dma((4,)), dma((4,)),
        ],
        compiler_params=pltpu.CompilerParams(
            collective_id=0, has_side_effects=True, vmem_limit_bytes=56 << 20
        ),
    )(
        traces, owner.reshape(32, W), patch_node.reshape(32, W), case_weights, smoothing, links, prior, stiffness
    )


def solution(mesh):
    in_specs = (
        P(("brick", "slab"), None),
        P(("brick", "slab"), None),
        P(("brick", "slab")),
        P(),
        P("brick", "slab"),
        P(None, "brick", "slab"),
        P("brick", "slab"),
        P("brick", "slab"),
    )
    out_specs = (P("brick", "slab"), P("brick", "slab"))
    return jax.shard_map(local, mesh=mesh, in_specs=in_specs, out_specs=out_specs, check_vma=False)
```

time: 77.8 us -> 66.6 us (0.86)
  Pallas kernels: 74 us -> 62.8 us
    pallas_call x1, Pallas kernels: 74 us -> 62.8 us  [local(): pl.pallas_call(kernel, out_shape=(jax.ShapeDtypeStruct((32, W), F32), jax...]
where the time goes in v2:
time: 66.6 us; the launch traced here: 66.3 us
  Pallas kernels  62.8 us (94%)
  local copies, waits for them, and re-layouts  2.89 us (4%)
    pallas_call x1, Pallas kernels, local(): pl.pallas_call(kernel, out_shape=(jax.ShapeDtypeStruct((32, W), F32), jax...  62.8 us
    unnamed x2, local copies, waits for them, and re-layouts  2.89 us

profile of v2, /device:TPU:1, one launch (start us, length us, event | category | flops | bytes accessed | tf_op | source)
XLA Modules:
  0.0 66.3 jit_solution(2105286582508860262)
XLA Ops:
  0.6 62.8 %shard_map.95 = (f32[32,128]{1,0:T(8,128)}, f32[256,128]{1,0:T(8,128)}) custom-call(bf16[4096,128]{1,0:T(8,128)(2,1)} %tr_hbm.1, s32[32,128]{1,0:T(8,128)} %bitcast.2, s32[32,128]{1,0:T(8,128)} %bitcast.3, s32[16]{0:T(128)} %cw_ref.1, f32[32,128]{1,0:T(8,128)} %sm_ref.1, s32[4,32,128]{2,1,0:T(8,128)} %lk_ref.1, f32[256,128]{1,0:T(8,128)} %prior_ref.1, ...), custom_call_target="tpu_custom_call" | custom-call | tf_op jit(solution)/shard_map/pallas_call | solution.py:500
  63.4 1.3 %copy.12 = f32[32,128]{1,0:T(8,128)} copy(f32[32,128]{1,0:T(8,128)} %get-tuple-element.4) | data formatting | bytes 32768
  64.7 1.6 %copy.13 = f32[256,128]{1,0:T(8,128)} copy(f32[256,128]{1,0:T(8,128)} %get-tuple-element.5) | data formatting | bytes 262144

commit v3 on v2

--- a/solution.py
+++ b/solution.py
@@ -18,9 +18,8 @@
 ROWS = 4096
 CAP = 64
 W = 128
-STRIDE = 37
-UNSTRIDE = 45
-BACK = 21
+STRIDE = 29
+UNSTRIDE = 53
 STEPS = 8
 PER = ND // STEPS
 DLO = 512
@@ -423,17 +422,14 @@
     core = lax.rem(s, 2)
     chip = b * 4 + s // 2
 
-    def back_copy(i):
-        t = lax.rem(chip + BACK * i, ND // 2)
-        return rcopy(
-            msg.at[pl.ds(t * 8, 8)], back.at[pl.ds(chip * 8, 8)], asend, arecv, (t // 4, 2 * lax.rem(t, 4) + core)
-        )
-
-    def go1(i, _):
-        back_copy(i).start()
-        return 0
-
-    lax.fori_loop(1, ND // 2, go1, 0)
+    far = sorted(range(1, 64), key=lambda o: -sum(min(d, 4 - d) for d in (o >> 4, (o >> 2) & 3, o & 3)))
+    cz, cx, cy = b >> 2, b & 3, s >> 1
+    for o in far:
+        tb = (((cz + (o >> 4)) & 3) << 2) + ((cx + ((o >> 2) & 3)) & 3)
+        ty = (cy + (o & 3)) & 3
+        rcopy(
+            msg.at[pl.ds((tb * 4 + ty) * 8, 8)], back.at[pl.ds(chip * 8, 8)], asend, arecv, (tb, 2 * ty + core)
+        ).start()
     here = pl.ds(pl.multiple_of(chip * 8, 8), 8)
     back[here, :] = msg[here, :]
     pltpu.make_async_copy(msg.at[pl.ds(0, 63 * 8)], back.at[pl.ds(0, 63 * 8)], arecv).wait()

time: 66.6 us -> 65.1 us (0.977)
  Pallas kernels: 62.8 us -> 61.3 us
    pallas_call x1, Pallas kernels: 62.8 us -> 61.3 us  [local(): pl.pallas_call(kernel, out_shape=(jax.ShapeDtypeStruct((32, W), F32), jax...]
where the time goes in v3:
time: 65.1 us; the launch traced here: 64.9 us
  Pallas kernels  61.3 us (94%)
  local copies, waits for them, and re-layouts  2.89 us (4%)
    pallas_call x1, Pallas kernels, local(): pl.pallas_call(kernel, out_shape=(jax.ShapeDtypeStruct((32, W), F32), jax...  61.3 us
    unnamed x2, local copies, waits for them, and re-layouts  2.89 us

profile of v3, /device:TPU:1, one launch (start us, length us, event | category | flops | bytes accessed | tf_op | source)
XLA Modules:
  0.0 64.9 jit_solution(5309869320071833887)
XLA Ops:
  0.6 61.3 %shard_map.95 = (f32[32,128]{1,0:T(8,128)}, f32[256,128]{1,0:T(8,128)}) custom-call(bf16[4096,128]{1,0:T(8,128)(2,1)} %tr_hbm.1, s32[32,128]{1,0:T(8,128)} %bitcast.2, s32[32,128]{1,0:T(8,128)} %bitcast.3, s32[16]{0:T(128)} %cw_ref.1, f32[32,128]{1,0:T(8,128)} %sm_ref.1, s32[4,32,128]{2,1,0:T(8,128)} %lk_ref.1, f32[256,128]{1,0:T(8,128)} %prior_ref.1, ...), custom_call_target="tpu_custom_call" | custom-call | tf_op jit(solution)/shard_map/pallas_call | solution.py:496
  62.0 1.3 %copy.12 = f32[32,128]{1,0:T(8,128)} copy(f32[32,128]{1,0:T(8,128)} %get-tuple-element.4) | data formatting | bytes 32768
  63.3 1.6 %copy.13 = f32[256,128]{1,0:T(8,128)} copy(f32[256,128]{1,0:T(8,128)} %get-tuple-element.5) | data formatting | bytes 262144

commit v4 on v3

--- a/solution.py
+++ b/solution.py
@@ -18,8 +18,8 @@
 ROWS = 4096
 CAP = 64
 W = 128
-STRIDE = 29
-UNSTRIDE = 53
+STRIDE = 13
+UNSTRIDE = 69
 STEPS = 8
 PER = ND // STEPS
 DLO = 512
@@ -57,8 +57,8 @@
     bar = pltpu.get_barrier_semaphore()
 
     def greet(i, _):
-        t = lax.rem(me + i, ND)
-        pl.semaphore_signal(bar, inc=1, device_id=(t // NS, lax.rem(t, NS)), device_id_type=MESH)
+        t = (me + i) & (ND - 1)
+        pl.semaphore_signal(bar, inc=1, device_id=(t >> 3, t & (NS - 1)), device_id_type=MESH)
         return 0
 
     lax.fori_loop(1, ND, greet, 0, unroll=4)
@@ -159,7 +159,7 @@
             c.start()
 
     def stage1_copy(d):
-        to = lax.rem(s + d, NS)
+        to = (s + d) & (NS - 1)
         return rcopy(
             labl.at[pl.ds(to * NB, NB)], r1.at[pl.ds(s * NB, NB)], lsend, lrecv, (b, to)
         )
@@ -200,7 +200,7 @@
         lax.fori_loop(1, NS, go, 0)
 
     def stage2_copy(d):
-        to = lax.rem(b + d, NB)
+        to = (b + d) & (NB - 1)
         return rcopy(
             r2.at[pl.ds(to * NS, NS)], ids.at[pl.ds(b * NS, NS)], l2send, l2recv, (to, s)
         )
@@ -218,10 +218,11 @@
 
         lax.fori_loop(1, NB, go, 0)
 
-    def trace_copy(i):
-        t = lax.rem(me + STRIDE * (i + 1), ND)
+    def trace_copy(j, n):
+        i = PER * j + n
+        t = (me + STRIDE * (i + 1)) & (ND - 1)
         return rcopy(
-            sendbuf.at[i], recv.at[i], tsend, trecv.at[i // PER], (t // NS, lax.rem(t, NS))
+            sendbuf.at[i], recv.at[i], tsend, trecv.at[j], (t >> 3, t & (NS - 1))
         )
 
     def fill_step(j):
@@ -237,10 +238,10 @@
 
     def dispatch(j, _):
         def go(i, _):
-            trace_copy(PER * (j - 1) + i).start()
+            trace_copy(j - 1, i).start()
             return 0
 
-        lax.fori_loop(0, PER, go, 0)
+        lax.fori_loop(0, PER, go, 0, unroll=4)
         fill_step(j)
 
         @pl.when(j == 1)
@@ -258,16 +259,16 @@
     lax.fori_loop(1, STEPS, dispatch, 0)
 
     def last(i, _):
-        trace_copy(PER * (STEPS - 1) + i).start()
-        return 0
-
-    lax.fori_loop(0, PER - 1, last, 0)
+        trace_copy(STEPS - 1, i).start()
+        return 0
+
+    lax.fori_loop(0, PER - 1, last, 0, unroll=5)
     pltpu.make_async_copy(sendbuf.at[ND - 1], recv.at[ND - 1], trecv.at[STEPS - 1]).start()
 
     pltpu.make_async_copy(r2.at[pl.ds(0, 15 * NS)], ids.at[pl.ds(0, 15 * NS)], l2recv).wait()
 
     def reorder(i, _):
-        src = lax.rem(me - STRIDE * (i + 1) + ND * STRIDE, ND)
+        src = (me - STRIDE * (i + 1) + ND * STRIDE) & (ND - 1)
         idrel[pl.ds(i, 1), :] = ids[pl.ds(src, 1), :]
         return 0
 

time: 65.1 us -> 63.6 us (0.977)
  Pallas kernels: 61.3 us -> 59.8 us
    pallas_call x1, Pallas kernels: 61.3 us -> 59.8 us  [local(): pl.pallas_call(kernel, out_shape=(jax.ShapeDtypeStruct((32, W), F32), jax...]
where the time goes in v4:
time: 63.6 us; the launch traced here: 63.3 us
  Pallas kernels  59.8 us (94%)
  local copies, waits for them, and re-layouts  2.89 us (5%)
  between operations  0.64 us (1%)
    pallas_call x1, Pallas kernels, local(): pl.pallas_call(kernel, out_shape=(jax.ShapeDtypeStruct((32, W), F32), jax...  59.8 us
    unnamed x2, local copies, waits for them, and re-layouts  2.89 us

profile of v4, /device:TPU:1, one launch (start us, length us, event | category | flops | bytes accessed | tf_op | source)
XLA Modules:
  0.0 63.3 jit_solution(9627777343389795517)
XLA Ops:
  0.6 59.8 %shard_map.95 = (f32[32,128]{1,0:T(8,128)}, f32[256,128]{1,0:T(8,128)}) custom-call(bf16[4096,128]{1,0:T(8,128)(2,1)} %tr_hbm.1, s32[32,128]{1,0:T(8,128)} %bitcast.2, s32[32,128]{1,0:T(8,128)} %bitcast.3, s32[16]{0:T(128)} %cw_ref.1, f32[32,128]{1,0:T(8,128)} %sm_ref.1, s32[4,32,128]{2,1,0:T(8,128)} %lk_ref.1, f32[256,128]{1,0:T(8,128)} %prior_ref.1, ...), custom_call_target="tpu_custom_call" | custom-call | tf_op jit(solution)/shard_map/pallas_call | solution.py:497
  60.4 1.3 %copy.12 = f32[32,128]{1,0:T(8,128)} copy(f32[32,128]{1,0:T(8,128)} %get-tuple-element.4) | data formatting | bytes 32768
  61.8 1.6 %copy.13 = f32[256,128]{1,0:T(8,128)} copy(f32[256,128]{1,0:T(8,128)} %get-tuple-element.5) | data formatting | bytes 262144

commit v5 on v4

--- a/solution.py
+++ b/solution.py
@@ -254,8 +254,8 @@
 
         return 0
 
+    fill_step(0)
     labels_stage1()
-    fill_step(0)
     lax.fori_loop(1, STEPS, dispatch, 0)
 
     def last(i, _):

time: 63.6 us -> 66 us (1.038)
  Pallas kernels: 59.8 us -> 62.2 us
    pallas_call x1, Pallas kernels: 59.8 us -> 62.2 us  [local(): pl.pallas_call(kernel, out_shape=(jax.ShapeDtypeStruct((32, W), F32), jax...]
where the time goes in v5:
time: 66 us; the launch traced here: 65.7 us
  Pallas kernels  62.2 us (94%)
  local copies, waits for them, and re-layouts  2.89 us (4%)
    pallas_call x1, Pallas kernels, local(): pl.pallas_call(kernel, out_shape=(jax.ShapeDtypeStruct((32, W), F32), jax...  62.2 us
    unnamed x2, local copies, waits for them, and re-layouts  2.89 us

profile of v5, /device:TPU:1, one launch (start us, length us, event | category | flops | bytes accessed | tf_op | source)
XLA Modules:
  0.0 65.7 jit_solution(13654172867283096724)
XLA Ops:
  0.6 62.2 %shard_map.95 = (f32[32,128]{1,0:T(8,128)}, f32[256,128]{1,0:T(8,128)}) custom-call(bf16[4096,128]{1,0:T(8,128)(2,1)} %tr_hbm.1, s32[32,128]{1,0:T(8,128)} %bitcast.2, s32[32,128]{1,0:T(8,128)} %bitcast.3, s32[16]{0:T(128)} %cw_ref.1, f32[32,128]{1,0:T(8,128)} %sm_ref.1, s32[4,32,128]{2,1,0:T(8,128)} %lk_ref.1, f32[256,128]{1,0:T(8,128)} %prior_ref.1, ...), custom_call_target="tpu_custom_call" | custom-call | tf_op jit(solution)/shard_map/pallas_call | solution.py:497
  62.8 1.3 %copy.12 = f32[32,128]{1,0:T(8,128)} copy(f32[32,128]{1,0:T(8,128)} %get-tuple-element.4) | data formatting | bytes 32768
  64.2 1.6 %copy.13 = f32[256,128]{1,0:T(8,128)} copy(f32[256,128]{1,0:T(8,128)} %get-tuple-element.5) | data formatting | bytes 262144
